TPU v7x, 512 devices: a whole 4x8x8 slice. The times are simulated.
512 devices in a mesh: slab: 64 (over z_hi, y, core), dp: 8 (over z_lo, x).
Axes of the slice: x: 4, y: 8, z: 8 (z_hi: 4, z_lo: 2; z = z_hi * 2 + z_lo), core: 2. Of those that a mesh axis runs over, the one named last changes fastest.
Arguments:
- universe: bfloat16 [8, 4, 256, 4, 512], P('dp', None, 'slab'), may hold values from -6 to 6
- cotangent: bfloat16 [8, 64, 64, 1, 128], P('dp', None, 'slab'), may hold values from -0.15625 to 0.15625
- conv1_weight: bfloat16 [32, 108], replicated, may hold values from -0.625 to 0.625
- conv1_bias: float32 [32], replicated, may hold values from -3 to 3
- conv2_weight: bfloat16 [64, 864], replicated, may hold values from -0.21875 to 0.21875
- conv2_bias: float32 [64], replicated, may hold values from -3 to 3
- owners: int32 [460, 1], replicated, may hold values from 0 to 7; in each aligned block of 460 rows (0 to 459, 460 to 919, ...) at most 138 rows name the same one
- accumulated: float32 [1104, 128], P('dp'), may hold values from -1 to 1
Outputs:
- features: bfloat16 [8, 64, 64, 1, 128], P('dp', None, 'slab')
- owned: float32 [1104, 128], P('dp')
Inputs may be any that keep to these rules, and one draw needn't show every extreme that they name: `owners`: each index of dp owns at most 138 blocks, exactly 138 for one of them, and at least one for each.
All inputs are finite; a program needn't handle non-finite values.
Results may differ from a plain program's by a relative error of at most 0.0014.
The roundings to bfloat16 on the way count: a program that leaves them out, or rounds other values in their place, can miss the bound.
Values may be sent and summed in bfloat16 or wider, within the bound.
No kernel may reach another device: no remote copies, remote signals or barrier semaphores. Data moves between devices by JAX's collectives and lax.ppermute only.
A program may use at most 64 MiB of HBM per device.

v0:
```python
import jax
import jax.numpy as jnp
from jax import lax
from jax.sharding import PartitionSpec as P

NB = 460
SLOPE = 0.3
OFFSETS = [
    (first, second, third) for first in range(3) for second in range(3) for third in range(3)
]


def with_halo(block, sides, width):
    for axis, dim in sides:
        count = lax.axis_size(axis)
        forward = [(i, i + 1) for i in range(count - 1)]
        forward.append((count - 1, 0))
        backward = [(target, source) for source, target in forward]
        low = lax.ppermute(
            lax.slice_in_dim(block, block.shape[dim] - width, None, axis=dim), axis, forward
        )
        high = lax.ppermute(lax.slice_in_dim(block, 0, width, axis=dim), axis, backward)
        block = jnp.concatenate([low, block, high], axis=dim)
    return block


def pad_sides(field):
    return jnp.pad(field, ((0, 0), (0, 0), (1, 1), (1, 1)))


def tap_stack(padded, deep_rows, high_rows, wide_rows, flipped):
    pieces = [
        padded[:, first : first + deep_rows, second : second + high_rows, third : third + wide_rows]
        for first, second, third in OFFSETS
    ]
    if flipped:
        pieces = pieces[::-1]
    stacked = jnp.stack(pieces, axis=0)
    return stacked.reshape(27 * padded.shape[0], deep_rows * high_rows * wide_rows)


def average(field):
    chans, deep_rows, high_rows, wide_rows = field.shape
    return field.reshape(chans, deep_rows // 2, 2, high_rows // 2, 2, wide_rows // 2, 2).mean(
        axis=(2, 4, 6)
    )


def spread_back(field):
    return jnp.repeat(jnp.repeat(jnp.repeat(field, 2, axis=1), 2, axis=2), 2, axis=3) * 0.125


def leaky_relu(value):
    return jnp.where(value > 0, value, SLOPE * value)


def slope_mask(value):
    return jnp.where(value > 0, 1.0, SLOPE)


def place_blocks(owners, blocks, ranks, capacity):
    owner_of = owners[:, 0]
    member = (owner_of[:, None] == jnp.arange(ranks, dtype=jnp.int32)[None, :]).astype(jnp.int32)
    before = jnp.cumsum(member, axis=0) - member
    slot_index = jnp.sum(before * member, axis=1)
    target = owner_of * capacity + slot_index
    placing = (jnp.arange(ranks * capacity, dtype=jnp.int32)[:, None] == target[None, :]).astype(
        jnp.float32
    )
    return jnp.dot(placing, blocks, precision=lax.Precision.HIGHEST)


def body(
    universe, cotangent, conv1_weight, conv1_bias, conv2_weight, conv2_bias, owners, accumulated
):
    field = universe[0]
    chans_in, deep_rows, high_rows, wide_rows = field.shape
    chan_one = conv1_weight.shape[0]
    chan_two = conv2_weight.shape[0]
    half_deep, half_high, half_wide = (deep_rows // 2, high_rows // 2, wide_rows // 2)
    extended = with_halo(field, (("slab", 1),), 1)
    cols_one = tap_stack(pad_sides(extended), deep_rows, high_rows, wide_rows, False)
    pre_one = (
        jnp.dot(conv1_weight, cols_one, preferred_element_type=jnp.float32) + conv1_bias[:, None]
    )
    pre_one = pre_one.reshape(chan_one, deep_rows, high_rows, wide_rows)
    pooled = average(leaky_relu(pre_one)).astype(jnp.bfloat16)
    rimmed = with_halo(pooled, (("slab", 1),), 1)
    cols_two = tap_stack(pad_sides(rimmed), half_deep, half_high, half_wide, False)
    pre_two = (
        jnp.dot(conv2_weight, cols_two, preferred_element_type=jnp.float32) + conv2_bias[:, None]
    )
    pre_two = pre_two.reshape(chan_two, half_deep, half_high, half_wide)
    feature = average(leaky_relu(pre_two)).astype(jnp.bfloat16)
    delta_two = (spread_back(cotangent[0].astype(jnp.float32)) * slope_mask(pre_two)).astype(
        jnp.bfloat16
    )
    flat_two = delta_two.reshape(chan_two, -1)
    grad_w2 = jnp.einsum("oc,kc->ok", flat_two, cols_two, preferred_element_type=jnp.float32)
    grad_b2 = jnp.sum(flat_two.astype(jnp.float32), axis=1)
    delta_rim = with_halo(delta_two, (("slab", 1),), 1)
    cols_back = tap_stack(pad_sides(delta_rim), half_deep, half_high, half_wide, True)
    weight_back = (
        conv2_weight.reshape(chan_two, 27, chan_one)
        .transpose(2, 1, 0)
        .reshape(chan_one, 27 * chan_two)
    )
    back_pooled = jnp.dot(weight_back, cols_back, preferred_element_type=jnp.float32)
    back_pooled = back_pooled.reshape(chan_one, half_deep, half_high, half_wide)
    delta_one = (spread_back(back_pooled) * slope_mask(pre_one)).astype(jnp.bfloat16)
    flat_one = delta_one.reshape(chan_one, -1)
    grad_w1 = jnp.einsum("oc,kc->ok", flat_one, cols_one, preferred_element_type=jnp.float32)
    grad_b1 = jnp.sum(flat_one.astype(jnp.float32), axis=1)
    vector = jnp.concatenate([grad_w1.reshape(-1), grad_b1, grad_w2.reshape(-1), grad_b2])
    blocks = jnp.pad(vector, (0, NB * 128 - vector.shape[0])).reshape(NB, 128)
    ranks = lax.axis_size("dp")
    capacity = accumulated.shape[0]
    totals = lax.psum(blocks, "slab")
    packed = place_blocks(owners, totals, ranks, capacity)
    mine = lax.psum_scatter(packed, "dp", scatter_dimension=0, tiled=True)
    owned = accumulated + mine
    return (feature[None], owned)


def solution(mesh):
    in_specs = (
        P("dp", None, "slab", None, None),
        P("dp", None, "slab", None, None),
        P(),
        P(),
        P(),
        P(),
        P(),
        P("dp", None),
    )
    out_specs = (P("dp", None, "slab", None, None), P("dp", None))
    return jax.shard_map(body, mesh=mesh, in_specs=in_specs, out_specs=out_specs, check_vma=False)
```

profile of v0, /device:TPU:64, one launch (start us, length us, event | category | flops | bytes accessed | tf_op | source)
XLA Modules:
  0.0 733.3 jit_solution(869186729282681174)
XLA Ops:
  8.0 1.9 collective-permute-start
  9.9 12.4 %collective-permute-start.1 = (bf16[4,1,4,512]{3,2,1,0:T(4,128)(2,1)S(1)}, bf16[4,1,4,512]{3,2,1,0:T(4,128)(2,1)S(1)}, u32[]{:S(2)}, u32[]{:S(2)}) collective-permute-start(bf16[4,1,4,512]{3,2,1,0:T(4,128)(2,1)S(1)} %get-tuple-element.22), channel_id=1, source_target_pairs={{8,0},{16,8},{24,16},{32,24},{40,32},{48,40},{56,48},{64,56},{72,6... | collective-permute-start | bytes 49160 | tf_op jit(solution)/shard_map/ppermute | solution.py:22
  23.7 1.1 reduce-window.6
  25.2 1.0 select_maximum_fusion.4
  29.0 1.4 constant_dynamic-update-slice_fusion.22
  36.0 1.5 constant_dynamic-update-slice_fusion.13
  43.1 1.4 constant_dynamic-update-slice_fusion.4
  47.4 3.8 reshape.172
  51.7 2.6 copy.90
  54.3 6.5 fusion.2
  62.3 1.9 collective-permute-start.2
  64.2 8.0 %collective-permute-start.3 = (bf16[32,1,2,256]{0,3,2,1:T(8,128)(2,1)}, bf16[32,1,2,256]{0,3,2,1:T(8,128)(2,1)}, u32[]{:S(2)}, u32[]{:S(2)}) collective-permute-start(bf16[32,1,2,256]{0,3,2,1:T(8,128)(2,1)} %get-tuple-element.18), channel_id=1, source_target_pairs={{8,0},{16,8},{24,16},{32,24},{40,32},{48,40},{56,48},{64,56},{72,6... | collective-permute-start | bytes 98312 | tf_op jit(solution)/shard_map/ppermute | solution.py:22
  72.4 0.9 broadcast_in_dim.46
  73.3 1.2 copy.101
  75.3 1.6 copy.94
  76.9 1.7 copy.96
  78.6 1.7 copy.97
  80.3 1.9 reshape.180
  82.2 1.2 select_maximum_fusion
  86.4 1.7 fusion.43
  90.3 0.8 fusion.38
  98.7 0.8 fusion.28
  101.0 1.7 fusion.25
  105.7 8.2 %copy.91 = bf16[27,32,2,2,256]{4,3,2,1,0:T(2,128)(2,1)} copy(bf16[27,32,2,2,256]{1,4,3,2,0:T(8,128)(2,1)} %fusion.20) | data formatting | bytes 3538944 | tf_op jit(solution)/shard_map/stack | solution.py:38
  113.9 5.2 reshape.174
  119.1 3.3 convert_reduce_fusion.1
  122.6 1.0 multiply_convert_fusion.4
  124.3 1.9 collective-permute-start.4
  126.3 7.9 %collective-permute-start.5 = (bf16[64,1,2,256]{3,2,1,0:T(2,128)(2,1)}, bf16[64,1,2,256]{3,2,1,0:T(2,128)(2,1)}, u32[]{:S(2)}, u32[]{:S(2)}) collective-permute-start(bf16[64,1,2,256]{3,2,1,0:T(2,128)(2,1)} %get-tuple-element.20), channel_id=1, source_target_pairs={{8,0},{16,8},{24,16},{32,24},{40,32},{48,40},{56,48},{64,56},{72,6... | collective-permute-start | bytes 196616 | tf_op jit(solution)/shard_map/ppermute | solution.py:22
  134.1 2.9 fusion.62
  137.3 1.8 reshape.182
  139.1 2.6 select_maximum_fusion.2
  141.7 1.0 constant_dynamic-update-slice_fusion.53
  142.7 1.0 constant_dynamic-update-slice_fusion.52
  144.4 1.0 constant_dynamic-update-slice_fusion.50
  145.4 1.6 constant_dynamic-update-slice_fusion.49
  147.8 0.9 constant_dynamic-update-slice_fusion.47
  148.6 0.9 constant_dynamic-update-slice_fusion.46
  150.3 1.0 constant_dynamic-update-slice_fusion.44
  151.2 1.0 constant_dynamic-update-slice_fusion.43
  152.2 0.8 constant_dynamic-update-slice_fusion.42
  153.0 1.0 constant_dynamic-update-slice_fusion.41
  154.8 0.8 constant_dynamic-update-slice_fusion.39
  155.5 0.9 constant_dynamic-update-slice_fusion.38
  156.4 0.9 constant_dynamic-update-slice_fusion.37
  158.1 1.0 constant_dynamic-update-slice_fusion.35
  159.0 1.0 constant_dynamic-update-slice_fusion.34
  160.0 0.8 constant_dynamic-update-slice_fusion.33
  160.8 1.0 constant_dynamic-update-slice_fusion.32
  161.8 1.6 constant_dynamic-update-slice_fusion.31
  164.2 0.9 constant_dynamic-update-slice_fusion.29
  165.0 0.9 constant_dynamic-update-slice_fusion.28
  166.6 8.9 %reshape.178 = bf16[1728,1024]{1,0:T(8,128)(2,1)} reshape(bf16[27,64,2,2,256]{4,3,2,1,0:T(2,128)(2,1)} %constant_dynamic-update-slice_fusion.27) | data formatting | bytes 7077888 | tf_op jit(solution)/shard_map/reshape | solution.py:39
  175.6 2.7 fusion.11
  178.8 3.4 broadcast_in_dim.44
  182.2 3.6 copy.99
  185.9 1.6 convert_reduce_fusion
  188.4 1.6 concatenate.39
  190.7 1.3 dynamic-slice.4
  193.3 498.6 %all-reduce.9.cloned.1.call-done = f32[460,128]{1,0:T(8,128)} async-done(((f32[460,128]{1,0:T(8,128)}), f32[460,128]{1,0:T(8,128)}) %all-reduce.9.cloned.1.call-update) | async-done | bytes 235536 | tf_op jit(solution)/shard_map/psum | solution.py:118
  691.9 2.1 fusion.3
  694.0 23.7 %fusion = f32[144,128]{1,0:T(8,128)S(1)} fusion(f32[1104,128]{1,0:T(8,128)S(1)} %fusion.3), kind=kCustom, calls=%all-reduce-scatter | all-reduce-scatter fusion | flops 147457 | bytes 641024
  717.7 1.9 collective-permute-start.6
  720.3 5.2 collective-permute-done.6
  (119 shorter events, 50.5 us)
Async XLA Ops:
  7.2 44.1 %copy-start = (bf16[32,108]{1,0:T(8,128)(2,1)S(1)}, bf16[32,108]{1,0:T(8,128)(2,1)}, u32[]{:S(2)}) copy-start(bf16[32,108]{1,0:T(8,128)(2,1)} %param.10) | copy-start | bytes 20740
  7.2 684.7 %all-reduce.9.cloned.1.call-start = ((), (), s32[]{:S(2)}) async-start(), calls=%async_computation | async-start | bytes 475136 | tf_op jit(solution)/shard_map/psum | solution.py:118
  8.0 17.2 %collective-permute-start = (bf16[4,1,4,512]{3,2,1,0:T(4,128)(2,1)S(1)}, bf16[4,1,4,512]{3,2,1,0:T(4,128)(2,1)S(1)}, u32[]{:S(2)}, u32[]{:S(2)}) collective-permute-start(bf16[4,1,4,512]{3,2,1,0:T(4,128)(2,1)S(1)} %get-tuple-element.21), channel_id=1, source_target_pairs={{0,8},{8,16},{16,24},{24,32},{32,40},{40,48},{48,56},{56,64},{64,7... | collective-permute-start | bytes 49160 | tf_op jit(solution)/shard_map/ppermute | solution.py:19
  9.9 15.3 %collective-permute-start.1 = (bf16[4,1,4,512]{3,2,1,0:T(4,128)(2,1)S(1)}, bf16[4,1,4,512]{3,2,1,0:T(4,128)(2,1)S(1)}, u32[]{:S(2)}, u32[]{:S(2)}) collective-permute-start(bf16[4,1,4,512]{3,2,1,0:T(4,128)(2,1)S(1)} %get-tuple-element.22), channel_id=1, source_target_pairs={{8,0},{16,8},{24,16},{32,24},{40,32},{48,40},{56,48},{64,56},{72,6... | collective-permute-start | bytes 49160 | tf_op jit(solution)/shard_map/ppermute | solution.py:22
  26.9 24.4 %copy-start.11 = (f32[32]{0:T(128)S(1)}, f32[32]{0:T(128)}, u32[]{:S(2)}) copy-start(f32[32]{0:T(128)} %param.11) | copy-start | bytes 388
  54.3 18.0 %copy-start.9 = (s32[460,1]{0,1:T(1,128)S(1)}, s32[460,1]{0,1:T(1,128)}, u32[]{:S(2)}) copy-start(s32[460,1]{0,1:T(1,128)} %param.14) | copy-start | bytes 5524
  60.7 0.8 copy-start.1
  62.3 19.8 %collective-permute-start.2 = (bf16[32,1,2,256]{0,3,2,1:T(8,128)(2,1)}, bf16[32,1,2,256]{0,3,2,1:T(8,128)(2,1)}, u32[]{:S(2)}, u32[]{:S(2)}) collective-permute-start(bf16[32,1,2,256]{0,3,2,1:T(8,128)(2,1)} %get-tuple-element.17), channel_id=1, source_target_pairs={{0,8},{8,16},{16,24},{24,32},{32,40},{40,48},{48,56},{56,64},{64,7... | collective-permute-start | bytes 98312 | tf_op jit(solution)/shard_map/ppermute | solution.py:19
  64.2 17.9 %collective-permute-start.3 = (bf16[32,1,2,256]{0,3,2,1:T(8,128)(2,1)}, bf16[32,1,2,256]{0,3,2,1:T(8,128)(2,1)}, u32[]{:S(2)}, u32[]{:S(2)}) collective-permute-start(bf16[32,1,2,256]{0,3,2,1:T(8,128)(2,1)} %get-tuple-element.18), channel_id=1, source_target_pairs={{8,0},{16,8},{24,16},{32,24},{40,32},{48,40},{56,48},{64,56},{72,6... | collective-permute-start | bytes 98312 | tf_op jit(solution)/shard_map/ppermute | solution.py:22
  83.4 10.8 %copy-start.2 = (f32[32,2,2,256]{0,3,2,1:T(8,128)S(1)}, f32[32,2,2,256]{0,3,2,1:T(8,128)}, u32[]{:S(2)}) copy-start(f32[32,2,2,256]{0,3,2,1:T(8,128)} %copy-done.1) | copy-start | bytes 393220
  113.9 5.2 copy-start.6
  113.9 5.2 copy-start.12
  124.3 14.8 %collective-permute-start.4 = (bf16[64,1,2,256]{3,2,1,0:T(2,128)(2,1)}, bf16[64,1,2,256]{3,2,1,0:T(2,128)(2,1)}, u32[]{:S(2)}, u32[]{:S(2)}) collective-permute-start(bf16[64,1,2,256]{3,2,1,0:T(2,128)(2,1)} %get-tuple-element.19), channel_id=1, source_target_pairs={{0,8},{8,16},{16,24},{24,32},{32,40},{40,48},{48,56},{56,64},{64,7... | collective-permute-start | bytes 196616 | tf_op jit(solution)/shard_map/ppermute | solution.py:19
  126.3 12.8 %collective-permute-start.5 = (bf16[64,1,2,256]{3,2,1,0:T(2,128)(2,1)}, bf16[64,1,2,256]{3,2,1,0:T(2,128)(2,1)}, u32[]{:S(2)}, u32[]{:S(2)}) collective-permute-start(bf16[64,1,2,256]{3,2,1,0:T(2,128)(2,1)} %get-tuple-element.20), channel_id=1, source_target_pairs={{8,0},{16,8},{24,16},{32,24},{40,32},{48,40},{56,48},{64,56},{72,6... | collective-permute-start | bytes 196616 | tf_op jit(solution)/shard_map/ppermute | solution.py:22
  137.2 16.7 %copy-start.5 = (f32[64,256]{1,0:T(8,128)S(1)}, f32[64,256]{1,0:T(8,128)}, u32[]{:S(2)}) copy-start(f32[64,256]{1,0:T(8,128)} %copy.94) | copy-start | bytes 196612
  166.6 8.9 %copy-start.7 = (bf16[32,1728]{1,0:T(8,128)(2,1)S(1)}, bf16[32,1728]{1,0:T(8,128)(2,1)}, u32[]{:S(2)}) copy-start(bf16[32,1728]{1,0:T(8,128)(2,1)} %reshape.180) | copy-start | bytes 331780
  185.9 2.5 copy-start.4
  185.9 2.5 copy-start.10
  185.9 6.7 copy-start.3
  187.5 538.3 %copy-start.8 = (f32[138,128]{1,0:T(8,128)S(1)}, f32[138,128]{1,0:T(8,128)}, u32[]{:S(2)}) copy-start(f32[138,128]{1,0:T(8,128)} %param.15) | copy-start | bytes 211972
  717.7 7.8 %collective-permute-start.6 = (f32[42,128]{1,0:T(8,128)S(1)}, f32[42,128]{1,0:T(8,128)S(1)}, u32[]{:S(2)}, u32[]{:S(2)}) collective-permute-start(f32[42,128]{1,0:T(8,128)S(1)} %slice.446), channel_id=1, source_target_pairs={{0,1},{1,2},{2,3},{3,4},{4,5},{5,6},{6,7},{8,9},{9,10},{10,11},{11... | collective-permute-start | bytes 64520
Sparse Core Ops, SparseCore 0:
  190.8 501.0 all-reduce.8
where the time goes:
time: 735 us; the launch traced here: 733 us
  waiting for transfers between devices  504 us (69%)
  local copies, waits for them, and re-layouts  114 us (16%)
  starting transfers between devices  36 us (5%)
  other arithmetic  28.8 us (4%)
  blocking collectives  23.7 us (3%)
  between operations  15.1 us (2%)
  matrix products  12.1 us (2%)
    psum x1, waiting for transfers between devices, body(): totals = lax.psum(blocks, 'slab')  499 us
    unnamed x101, local copies, waits for them, and re-layouts  60 us
    ppermute x3, starting transfers between devices, with_halo(): lax.ppermute(lax.slice_in_dim(block, 0, width, axis=dim), axis, backward)  28.3 us
    unnamed x1, blocking collectives  23.7 us
    reshape x3, local copies, waits for them, and re-layouts, tap_stack(): stacked.reshape(27 * padded.shape[0], deep_rows * high_rows * wide_rows)  17.9 us
  transfers between devices with their start and end apart: 8, of which 2 were waited for; matrix products, arithmetic and copies ran while one was open for 3% of the time, Pallas kernels for 0%

commit v1 on v0

--- a/solution.py
+++ b/solution.py
@@ -115,7 +115,7 @@
     blocks = jnp.pad(vector, (0, NB * 128 - vector.shape[0])).reshape(NB, 128)
     ranks = lax.axis_size("dp")
     capacity = accumulated.shape[0]
-    totals = lax.psum(blocks, "slab")
+    totals = jnp.sum(lax.all_gather(blocks, "slab"), axis=0)
     packed = place_blocks(owners, totals, ranks, capacity)
     mine = lax.psum_scatter(packed, "dp", scatter_dimension=0, tiled=True)
     owned = accumulated + mine

time: 735 us -> 364 us (0.50)
  waiting for transfers between devices: 504 us -> 129 us
    psum x1 -> x0, waiting for transfers between devices: 499 us -> none  [body(): totals = lax.psum(blocks, 'slab')]
    all_gather x0 -> x1, waiting for transfers between devices: none -> 124 us  [body(): totals = jnp.sum(lax.all_gather(blocks, 'slab'), axis=0)]
  transfers between devices with their start and end apart: 8 -> 8, of which waited for: 2 -> 3; matrix products, arithmetic and copies ran while one was open for 3% -> 5% of each run, Pallas kernels for 0% -> 0%
where the time goes in v1:
time: 364 us; the launch traced here: 363 us
  waiting for transfers between devices  129 us (35%)
  local copies, waits for them, and re-layouts  114 us (31%)
  starting transfers between devices  37.5 us (10%)
  other arithmetic  33.4 us (9%)
  blocking collectives  23.1 us (6%)
  between operations  15.1 us (4%)
  matrix products  10.7 us (3%)
    all_gather x1, waiting for transfers between devices, body(): totals = jnp.sum(lax.all_gather(blocks, 'slab'), axis=0)  124 us
    unnamed x101, local copies, waits for them, and re-layouts  60 us
    ppermute x3, starting transfers between devices, with_halo(): lax.ppermute(lax.slice_in_dim(block, 0, width, axis=dim), axis, backward)  28.3 us
    unnamed x1, blocking collectives  23.1 us
    reshape x3, local copies, waits for them, and re-layouts, tap_stack(): stacked.reshape(27 * padded.shape[0], deep_rows * high_rows * wide_rows)  17.9 us
    unnamed x8, other arithmetic  11 us
    another operation x4, local copies, waits for them, and re-layouts, tap_stack(): stacked = jnp.stack(pieces, axis=0)  10.5 us
  transfers between devices with their start and end apart: 8, of which 3 were waited for; matrix products, arithmetic and copies ran while one was open for 5% of the time, Pallas kernels for 0%

profile of v1, /device:TPU:64, one launch (start us, length us, event | category | flops | bytes accessed | tf_op | source)
XLA Modules:
  0.0 362.8 jit_solution(7889948540648993306)
XLA Ops:
  8.0 1.9 collective-permute-start
  9.9 12.4 %collective-permute-start.1 = (bf16[4,1,4,512]{3,2,1,0:T(4,128)(2,1)S(1)}, bf16[4,1,4,512]{3,2,1,0:T(4,128)(2,1)S(1)}, u32[]{:S(2)}, u32[]{:S(2)}) collective-permute-start(bf16[4,1,4,512]{3,2,1,0:T(4,128)(2,1)S(1)} %get-tuple-element.22), channel_id=1, source_target_pairs={{8,0},{16,8},{24,16},{32,24},{40,32},{48,40},{56,48},{64,56},{72,6... | collective-permute-start | bytes 49160 | tf_op jit(solution)/shard_map/ppermute | solution.py:22
  22.3 1.4 collective-permute-done.1
  23.7 1.0 select_maximum_fusion.4
  27.5 1.4 constant_dynamic-update-slice_fusion.22
  34.5 1.5 constant_dynamic-update-slice_fusion.13
  41.6 1.4 constant_dynamic-update-slice_fusion.4
  45.9 3.8 %reshape.169 = bf16[108,8192]{1,0:T(8,128)(2,1)S(1)} reshape(bf16[27,4,4,4,512]{4,3,2,1,0:T(4,128)(2,1)} %constant_dynamic-update-slice_fusion) | data formatting | bytes 3538944 | tf_op jit(solution)/shard_map/reshape | solution.py:39
  50.2 2.6 copy.90
  52.8 6.5 %fusion.2 = f32[32,2,2,256]{0,3,2,1:T(8,128)S(1)} fusion(f32[32,2,2,2,2,256,2]{0,6,5,4,3,2,1:T(2,128)} %bitcast.360), kind=kLoop, calls=%fused_computation.3 | loop fusion | flops 1015808 | bytes 1179648 | tf_op jit(solution)/shard_map/reduce_sum | solution.py:44
  60.8 1.9 collective-permute-start.2
  62.7 8.0 %collective-permute-start.3 = (bf16[32,1,2,256]{0,3,2,1:T(8,128)(2,1)}, bf16[32,1,2,256]{0,3,2,1:T(8,128)(2,1)}, u32[]{:S(2)}, u32[]{:S(2)}) collective-permute-start(bf16[32,1,2,256]{0,3,2,1:T(8,128)(2,1)} %get-tuple-element.18), channel_id=1, source_target_pairs={{8,0},{16,8},{24,16},{32,24},{40,32},{48,40},{56,48},{64,56},{72,6... | collective-permute-start | bytes 98312 | tf_op jit(solution)/shard_map/ppermute | solution.py:22
  70.9 0.9 broadcast_in_dim.46
  71.8 1.2 copy.101
  73.7 1.6 copy.94
  75.4 1.7 copy.96
  77.1 1.7 copy.97
  78.8 1.9 reshape.177
  80.7 1.2 select_maximum_fusion
  84.9 1.7 fusion.43
  88.8 0.8 fusion.38
  97.2 0.8 fusion.28
  99.5 1.7 fusion.25
  104.2 8.2 %copy.91 = bf16[27,32,2,2,256]{4,3,2,1,0:T(2,128)(2,1)} copy(bf16[27,32,2,2,256]{1,4,3,2,0:T(8,128)(2,1)} %fusion.20) | data formatting | bytes 3538944 | tf_op jit(solution)/shard_map/stack | solution.py:38
  112.4 5.2 %reshape.171 = bf16[864,1024]{1,0:T(8,128)(2,1)} reshape(bf16[27,32,2,2,256]{4,3,2,1,0:T(2,128)(2,1)} %copy.91) | data formatting | bytes 3538944 | tf_op jit(solution)/shard_map/reshape | solution.py:39
  117.6 2.8 convert_reduce_fusion.1
  120.6 1.0 multiply_convert_fusion.4
  122.3 1.9 collective-permute-start.4
  124.3 7.9 %collective-permute-start.5 = (bf16[64,1,2,256]{3,2,1,0:T(2,128)(2,1)}, bf16[64,1,2,256]{3,2,1,0:T(2,128)(2,1)}, u32[]{:S(2)}, u32[]{:S(2)}) collective-permute-start(bf16[64,1,2,256]{3,2,1,0:T(2,128)(2,1)} %get-tuple-element.20), channel_id=1, source_target_pairs={{8,0},{16,8},{24,16},{32,24},{40,32},{48,40},{56,48},{64,56},{72,6... | collective-permute-start | bytes 196616 | tf_op jit(solution)/shard_map/ppermute | solution.py:22
  132.1 2.9 fusion.62
  135.3 1.8 reshape.179
  137.1 2.6 select_maximum_fusion.2
  139.7 1.0 constant_dynamic-update-slice_fusion.53
  140.7 1.0 constant_dynamic-update-slice_fusion.52
  142.4 1.0 constant_dynamic-update-slice_fusion.50
  143.4 1.6 constant_dynamic-update-slice_fusion.49
  145.8 0.9 constant_dynamic-update-slice_fusion.47
  146.7 0.9 constant_dynamic-update-slice_fusion.46
  148.3 1.0 constant_dynamic-update-slice_fusion.44
  149.3 1.0 constant_dynamic-update-slice_fusion.43
  151.0 1.0 constant_dynamic-update-slice_fusion.41
  152.8 0.8 constant_dynamic-update-slice_fusion.39
  153.6 0.9 constant_dynamic-update-slice_fusion.38
  154.4 0.9 constant_dynamic-update-slice_fusion.37
  156.1 1.0 constant_dynamic-update-slice_fusion.35
  157.0 1.0 constant_dynamic-update-slice_fusion.34
  158.8 1.0 constant_dynamic-update-slice_fusion.32
  159.8 1.6 constant_dynamic-update-slice_fusion.31
  162.2 0.9 constant_dynamic-update-slice_fusion.29
  163.1 0.9 constant_dynamic-update-slice_fusion.28
  164.7 8.9 %reshape.175 = bf16[1728,1024]{1,0:T(8,128)(2,1)} reshape(bf16[27,64,2,2,256]{4,3,2,1,0:T(2,128)(2,1)} %constant_dynamic-update-slice_fusion.27) | data formatting | bytes 7077888 | tf_op jit(solution)/shard_map/reshape | solution.py:39
  173.6 2.7 fusion.11
  176.9 3.4 broadcast_in_dim.44
  180.3 3.6 copy.99
  183.9 1.6 convert_reduce_fusion
  186.4 1.6 concatenate.39
  188.7 1.1 reduce-window.6
  190.1 1.3 dynamic-slice.4
  192.9 123.9 %all-gather.2.cloned.1.call-done = f32[64,460,128]{2,1,0:T(8,128)} async-done(((f32[1,460,128]{2,1,0:T(8,128)}), f32[64,460,128]{2,1,0:T(8,128)}) %all-gather.2.cloned.1.call-update) | async-done | bytes 15073296 | tf_op jit(solution)/shard_map/all_gather | solution.py:118
  316.8 6.0 %reduce_sum.59 = f32[460,128]{1,0:T(8,128)S(1)} reduce(f32[64,460,128]{2,1,0:T(8,128)} %all-gather.2.cloned.1.call-done, f32[]{:T(128)} %constant.9.clone.1), dimensions={0}, to_apply=%region_7.8 | reduce | flops 3709440 | bytes 15308804 | tf_op jit(solution)/shard_map/reduce_sum | solution.py:118
  322.9 1.2 fusion.3
  324.0 23.1 %fusion = f32[144,128]{1,0:T(8,128)S(1)} fusion(f32[1104,128]{1,0:T(8,128)S(1)} %fusion.3), kind=kCustom, calls=%all-reduce-scatter | all-reduce-scatter fusion | flops 147457 | bytes 641024
  347.2 3.5 collective-permute-start.6
  351.4 3.6 %collective-permute-done.6 = f32[42,128]{1,0:T(8,128)S(1)} collective-permute-done((f32[42,128]{1,0:T(8,128)S(1)}, f32[42,128]{1,0:T(8,128)S(1)}, u32[]{:S(2)}, u32[]{:S(2)}) %collective-permute-start.6) | collective-permute-done | bytes 21536
  (120 shorter events, 50.7 us)
Async XLA Ops:
  7.2 42.6 %copy-start = (bf16[32,108]{1,0:T(8,128)(2,1)S(1)}, bf16[32,108]{1,0:T(8,128)(2,1)}, u32[]{:S(2)}) copy-start(bf16[32,108]{1,0:T(8,128)(2,1)} %param.10) | copy-start | bytes 20740
  7.2 309.7 %all-gather.2.cloned.1.call-start = ((), (), s32[]{:S(2)}) async-start(), calls=%async_computation | async-start | bytes 15441920 | tf_op jit(solution)/shard_map/all_gather | solution.py:118
  8.0 14.3 %collective-permute-start = (bf16[4,1,4,512]{3,2,1,0:T(4,128)(2,1)S(1)}, bf16[4,1,4,512]{3,2,1,0:T(4,128)(2,1)S(1)}, u32[]{:S(2)}, u32[]{:S(2)}) collective-permute-start(bf16[4,1,4,512]{3,2,1,0:T(4,128)(2,1)S(1)} %get-tuple-element.21), channel_id=1, source_target_pairs={{0,8},{8,16},{16,24},{24,32},{32,40},{40,48},{48,56},{56,64},{64,7... | collective-permute-start | bytes 49160 | tf_op jit(solution)/shard_map/ppermute | solution.py:19
  9.9 13.8 %collective-permute-start.1 = (bf16[4,1,4,512]{3,2,1,0:T(4,128)(2,1)S(1)}, bf16[4,1,4,512]{3,2,1,0:T(4,128)(2,1)S(1)}, u32[]{:S(2)}, u32[]{:S(2)}) collective-permute-start(bf16[4,1,4,512]{3,2,1,0:T(4,128)(2,1)S(1)} %get-tuple-element.22), channel_id=1, source_target_pairs={{8,0},{16,8},{24,16},{32,24},{40,32},{48,40},{56,48},{64,56},{72,6... | collective-permute-start | bytes 49160 | tf_op jit(solution)/shard_map/ppermute | solution.py:22
  25.4 24.4 %copy-start.11 = (f32[32]{0:T(128)S(1)}, f32[32]{0:T(128)}, u32[]{:S(2)}) copy-start(f32[32]{0:T(128)} %param.11) | copy-start | bytes 388
  52.8 18.0 %copy-start.10 = (bf16[1,64,1,1,128]{4,1,3,2,0:T(8,128)(2,1)S(1)}, bf16[1,64,1,1,128]{4,1,3,2,0:T(8,128)(2,1)}, u32[]{:S(2)}) copy-start(bf16[1,64,1,1,128]{4,1,3,2,0:T(8,128)(2,1)} %param.9) | copy-start | bytes 49156
  59.2 0.8 copy-start.1
  60.8 19.8 %collective-permute-start.2 = (bf16[32,1,2,256]{0,3,2,1:T(8,128)(2,1)}, bf16[32,1,2,256]{0,3,2,1:T(8,128)(2,1)}, u32[]{:S(2)}, u32[]{:S(2)}) collective-permute-start(bf16[32,1,2,256]{0,3,2,1:T(8,128)(2,1)} %get-tuple-element.17), channel_id=1, source_target_pairs={{0,8},{8,16},{16,24},{24,32},{32,40},{40,48},{48,56},{56,64},{64,7... | collective-permute-start | bytes 98312 | tf_op jit(solution)/shard_map/ppermute | solution.py:19
  62.7 17.9 %collective-permute-start.3 = (bf16[32,1,2,256]{0,3,2,1:T(8,128)(2,1)}, bf16[32,1,2,256]{0,3,2,1:T(8,128)(2,1)}, u32[]{:S(2)}, u32[]{:S(2)}) collective-permute-start(bf16[32,1,2,256]{0,3,2,1:T(8,128)(2,1)} %get-tuple-element.18), channel_id=1, source_target_pairs={{8,0},{16,8},{24,16},{32,24},{40,32},{48,40},{56,48},{64,56},{72,6... | collective-permute-start | bytes 98312 | tf_op jit(solution)/shard_map/ppermute | solution.py:22
  81.9 10.8 %copy-start.2 = (f32[32,2,2,256]{0,3,2,1:T(8,128)S(1)}, f32[32,2,2,256]{0,3,2,1:T(8,128)}, u32[]{:S(2)}) copy-start(f32[32,2,2,256]{0,3,2,1:T(8,128)} %copy-done.1) | copy-start | bytes 393220
  112.4 5.2 %copy-start.6 = (bf16[64,864]{1,0:T(8,128)(2,1)S(1)}, bf16[64,864]{1,0:T(8,128)(2,1)}, u32[]{:S(2)}) copy-start(bf16[64,864]{1,0:T(8,128)(2,1)} %param.12) | copy-start | bytes 331780
  112.4 5.2 %copy-start.12 = (f32[64]{0:T(128)S(1)}, f32[64]{0:T(128)}, u32[]{:S(2)}) copy-start(f32[64]{0:T(128)} %param.13) | copy-start | bytes 772
  122.3 14.8 %collective-permute-start.4 = (bf16[64,1,2,256]{3,2,1,0:T(2,128)(2,1)}, bf16[64,1,2,256]{3,2,1,0:T(2,128)(2,1)}, u32[]{:S(2)}, u32[]{:S(2)}) collective-permute-start(bf16[64,1,2,256]{3,2,1,0:T(2,128)(2,1)} %get-tuple-element.19), channel_id=1, source_target_pairs={{0,8},{8,16},{16,24},{24,32},{32,40},{40,48},{48,56},{56,64},{64,7... | collective-permute-start | bytes 196616 | tf_op jit(solution)/shard_map/ppermute | solution.py:19
  124.3 12.9 %collective-permute-start.5 = (bf16[64,1,2,256]{3,2,1,0:T(2,128)(2,1)}, bf16[64,1,2,256]{3,2,1,0:T(2,128)(2,1)}, u32[]{:S(2)}, u32[]{:S(2)}) collective-permute-start(bf16[64,1,2,256]{3,2,1,0:T(2,128)(2,1)} %get-tuple-element.20), channel_id=1, source_target_pairs={{8,0},{16,8},{24,16},{32,24},{40,32},{48,40},{56,48},{64,56},{72,6... | collective-permute-start | bytes 196616 | tf_op jit(solution)/shard_map/ppermute | solution.py:22
  135.2 16.8 %copy-start.5 = (f32[64,256]{1,0:T(8,128)S(1)}, f32[64,256]{1,0:T(8,128)}, u32[]{:S(2)}) copy-start(f32[64,256]{1,0:T(8,128)} %copy.94) | copy-start | bytes 196612
  164.7 8.9 %copy-start.7 = (bf16[32,1728]{1,0:T(8,128)(2,1)S(1)}, bf16[32,1728]{1,0:T(8,128)(2,1)}, u32[]{:S(2)}) copy-start(bf16[32,1728]{1,0:T(8,128)(2,1)} %reshape.177) | copy-start | bytes 331780
  183.9 2.5 copy-start.4
  183.9 4.8 %copy-start.9 = (s32[460,1]{0,1:T(1,128)S(1)}, s32[460,1]{0,1:T(1,128)}, u32[]{:S(2)}) copy-start(s32[460,1]{0,1:T(1,128)} %param.14) | copy-start | bytes 5524
  183.9 8.3 %copy-start.3 = (f32[64,1024]{1,0:T(8,128)S(1)}, f32[64,1024]{1,0:T(8,128)}, u32[]{:S(2)}) copy-start(f32[64,1024]{1,0:T(8,128)} %get-tuple-element.23) | copy-start | bytes 786436
  192.9 162.4 %copy-start.8 = (f32[138,128]{1,0:T(8,128)S(1)}, f32[138,128]{1,0:T(8,128)}, u32[]{:S(2)}) copy-start(f32[138,128]{1,0:T(8,128)} %param.15) | copy-start | bytes 211972
  347.2 7.8 %collective-permute-start.6 = (f32[42,128]{1,0:T(8,128)S(1)}, f32[42,128]{1,0:T(8,128)S(1)}, u32[]{:S(2)}, u32[]{:S(2)}) collective-permute-start(f32[42,128]{1,0:T(8,128)S(1)} %slice.446), channel_id=1, source_target_pairs={{0,1},{1,2},{2,3},{3,4},{4,5},{5,6},{6,7},{8,9},{9,10},{10,11},{11... | collective-permute-start | bytes 64520
Sparse Core Ops, SparseCore 0:
  188.8 128.0 all-gather.1
